TPU v7x, 256 devices: a whole 4x4x8 slice. The times are simulated.
256 devices in a mesh: seq: 32 (over z_hi, y, core), pair: 8 (over z_lo, x).
Axes of the slice: x: 4, y: 4, z: 8 (z_hi: 4, z_lo: 2; z = z_hi * 2 + z_lo), core: 2. Of those that a mesh axis runs over, the one named last changes fastest.
Arguments:
- student: float32 [20480, 1408], P('seq'), may hold values from -640 to 640
- teacher: float32 [20480, 1408], P('seq'), may hold values from -640 to 640
Outputs:
- student_grad: float32 [20480, 1408], P('seq')
All inputs are finite; a program needn't handle non-finite values.
Results may differ from a plain program's by a relative error of at most 0.0059.
Values may be sent and summed in bfloat16 or wider, within the bound.
A program may use at most 64 MiB of HBM per device.

v0:
```python
import math
import jax
import jax.numpy as jnp
from jax import lax
from jax.sharding import PartitionSpec as P


def from_behind(block, axis, distance):
    devices = range(lax.axis_size(axis))
    route = [((i - distance) % len(devices), i) for i in devices]
    return lax.ppermute(block, axis, route)


def normalize(values, width):
    scale = lax.rsqrt(jnp.sum(values * values, axis=1, keepdims=True) + width * 1e-06)
    return (scale, values * scale)


def relation_tile(own_s, own_t, partner, margin, weight):
    contract = (((1,), (1,)), ((), ()))
    s_rel = lax.dot_general(own_s, partner[0], contract, preferred_element_type=jnp.float32)
    t_rel = lax.dot_general(own_t, partner[1], contract, preferred_element_type=jnp.float32)
    delta = s_rel - t_rel
    shrink = jnp.maximum(delta - margin, 0.0) + jnp.minimum(delta + margin, 0.0)
    relation = (weight * shrink).astype(jnp.bfloat16)
    return jnp.dot(relation, partner[0], preferred_element_type=jnp.float32)


def finish_rows(scale, unit, unit_grad):
    dotted = jnp.sum(unit * unit_grad, axis=1, keepdims=True)
    return scale * (unit_grad - unit * dotted)


def local(student, teacher):
    rows, width = student.shape
    seq_count = lax.axis_size("seq")
    pair_count = lax.axis_size("pair")
    block_count = seq_count // pair_count
    bit_count = pair_count.bit_length() - 1
    pair_index = lax.axis_index("pair")
    margin = 0.75 / math.sqrt(width)
    weight = 64.0 * width / math.sqrt(rows * seq_count)
    s_scale, s_unit = normalize(student, width)
    t_scale, t_unit = normalize(teacher, width)
    s_half = s_unit.astype(jnp.bfloat16)
    t_half = t_unit.astype(jnp.bfloat16)
    partner = jnp.stack([s_half, t_half])

    def tile(block):
        return relation_tile(s_half, t_half, block, margin, weight)

    for bit in range(bit_count):
        moved = from_behind(partner, "seq", 1 << bit)
        partner = jnp.where(pair_index // (1 << bit) % 2 == 1, moved, partner)

    def advance(step, carry):
        block, total = carry
        block = from_behind(block, "seq", pair_count)
        return (block, total + tile(block))

    partial_value = tile(partner)
    partner, partial_value = lax.fori_loop(0, block_count - 1, advance, (partner, partial_value))
    unit_grad = lax.psum(partial_value, "pair")
    return finish_rows(s_scale, s_unit, unit_grad)


def solution(mesh):
    placed = (P("seq", None), P("seq", None))
    return jax.shard_map(
        local, mesh=mesh, in_specs=placed, out_specs=P("seq", None), check_vma=False
    )
```

profile of v0, /device:TPU:1, one launch (start us, length us, event | category | flops | bytes accessed | tf_op | source)
XLA Modules:
  0.0 1078.7 jit_solution(164027926578918337)
XLA Ops:
  6.5 2.5 multiply_reduce_fusion.1
  13.6 2.7 collective-permute-start.1
  16.3 39.4 %collective-permute-done.1 = bf16[2,640,1408]{2,1,0:T(8,128)(2,1)} collective-permute-done((bf16[2,640,1408]{2,1,0:T(8,128)(2,1)}, bf16[2,640,1408]{2,1,0:T(8,128)(2,1)}, u32[]{:S(2)}, u32[]{:S(2)}) %collective-permute-start.1) | collective-permute-done | bytes 3604512 | tf_op jit(solution)/shard_map/ppermute | solution.py:11
  55.8 3.8 broadcast_select_fusion
  60.8 179.3 %collective-permute-done.2 = bf16[2,640,1408]{2,1,0:T(8,128)(2,1)} collective-permute-done((bf16[2,640,1408]{2,1,0:T(8,128)(2,1)}, bf16[2,640,1408]{2,1,0:T(8,128)(2,1)}, u32[]{:S(2)}, u32[]{:S(2)}) %collective-permute-start.2) | collective-permute-done | bytes 3604512 | tf_op jit(solution)/shard_map/ppermute | solution.py:11
  240.2 3.3 broadcast_select_fusion.1
  243.4 161.1 %collective-permute-done.3 = bf16[2,640,1408]{2,1,0:T(8,128)(2,1)} collective-permute-done((bf16[2,640,1408]{2,1,0:T(8,128)(2,1)}, bf16[2,640,1408]{2,1,0:T(8,128)(2,1)}, u32[]{:S(2)}, u32[]{:S(2)}) %collective-permute-start.3) | collective-permute-done | bytes 3604512 | tf_op jit(solution)/shard_map/ppermute | solution.py:11
  404.5 2.4 broadcast_select_fusion.2
  410.4 8.1 fusion.11
  418.5 514.4 %while.14 = (s32[]{:T(128)}, bf16[2,640,1408]{2,1,0:T(8,128)(2,1)}, f32[640,1408]{1,0:T(8,128)}, bf16[640,1408]{1,0:T(8,128)(2,1)}, bf16[640,1408]{1,0:T(8,128)(2,1)S(1)}, /*index=5*/s32[]{:T(128)}) while((s32[]{:T(128)}, bf16[2,640,1408]{2,1,0:T(8,128)(2,1)}, f32[640,1408]{1,0:T(8,128)}, bf16[640,1408]{1,0:T(8,128)(2,1)}, ...), condition=%wide.region_3.4_spmd, body=%wide.region_2.3_spmd.sunk | while | flops 3464478720 | bytes 41123948 | solution.py:62
  418.5 303.4 %collective-permute-done = bf16[2,640,1408]{2,1,0:T(8,128)(2,1)} collective-permute-done((bf16[2,640,1408]{2,1,0:T(8,128)(2,1)}, bf16[2,640,1408]{2,1,0:T(8,128)(2,1)}, u32[]{:S(2)}, u32[]{:S(2)}) %collective-permute-start) | collective-permute-done | bytes 3604512 | tf_op jit(solution)/shard_map/while/body/eval_jaxpr/ppermute | solution.py:11
  721.9 4.1 copy.10
  726.0 3.2 fusion.30
  729.1 9.1 convolution_add_fusion.2
  740.5 79.2 %collective-permute-done = bf16[2,640,1408]{2,1,0:T(8,128)(2,1)} collective-permute-done((bf16[2,640,1408]{2,1,0:T(8,128)(2,1)}, bf16[2,640,1408]{2,1,0:T(8,128)(2,1)}, u32[]{:S(2)}, u32[]{:S(2)}) %collective-permute-start) | collective-permute-done | bytes 3604512 | tf_op jit(solution)/shard_map/while/body/eval_jaxpr/ppermute | solution.py:11
  819.6 4.1 copy.10
  823.7 3.2 fusion.30
  826.9 9.1 convolution_add_fusion.2
  837.1 79.4 %collective-permute-done = bf16[2,640,1408]{2,1,0:T(8,128)(2,1)} collective-permute-done((bf16[2,640,1408]{2,1,0:T(8,128)(2,1)}, bf16[2,640,1408]{2,1,0:T(8,128)(2,1)}, u32[]{:S(2)}, u32[]{:S(2)}) %collective-permute-start) | collective-permute-done | bytes 3604512 | tf_op jit(solution)/shard_map/while/body/eval_jaxpr/ppermute | solution.py:11
  916.5 4.1 copy.10
  920.6 3.2 fusion.30
  923.8 9.1 convolution_add_fusion.2
  932.9 131.2 %all-reduce.2.cloned.1.call-done = f32[640,1408]{1,0:T(8,128)} async-done(((f32[640,1408]{1,0:T(8,128)}), f32[640,1408]{1,0:T(8,128)}) %all-reduce.2.cloned.1.call-update) | async-done | bytes 3604496 | tf_op jit(solution)/shard_map/psum | solution.py:63
  1064.2 3.7 multiply_reduce_fusion
  (26 shorter events, 16.5 us)
Async XLA Ops:
  6.5 1057.7 %all-reduce.2.cloned.1.call-start = ((), (), s32[]{:S(2)}) async-start(), calls=%async_computation | async-start | bytes 7208960 | tf_op jit(solution)/shard_map/psum | solution.py:63
  6.5 3.1 copy-start
  6.5 4.2 copy-start.3
  11.2 2.4 copy-start.2
  13.6 42.1 %collective-permute-start.1 = (bf16[2,640,1408]{2,1,0:T(8,128)(2,1)}, bf16[2,640,1408]{2,1,0:T(8,128)(2,1)}, u32[]{:S(2)}, u32[]{:S(2)}) collective-permute-start(bf16[2,640,1408]{2,1,0:T(8,128)(2,1)} %pad_maximum_fusion), channel_id=1, source_target_pairs={{248,0},{0,8},{8,16},{16,24},{24,32},{32,40},{40,48},{48,56},{56,6... | collective-permute-start | bytes 10813448 | tf_op jit(solution)/shard_map/ppermute | solution.py:11
  59.5 180.6 %collective-permute-start.2 = (bf16[2,640,1408]{2,1,0:T(8,128)(2,1)}, bf16[2,640,1408]{2,1,0:T(8,128)(2,1)}, u32[]{:S(2)}, u32[]{:S(2)}) collective-permute-start(bf16[2,640,1408]{2,1,0:T(8,128)(2,1)} %broadcast_select_fusion), channel_id=1, source_target_pairs={{240,0},{248,8},{0,16},{8,24},{16,32},{24,40},{32,48},{40,56},{48,... | collective-permute-start | bytes 10813448 | tf_op jit(solution)/shard_map/ppermute | solution.py:11
  243.4 161.1 %collective-permute-start.3 = (bf16[2,640,1408]{2,1,0:T(8,128)(2,1)}, bf16[2,640,1408]{2,1,0:T(8,128)(2,1)}, u32[]{:S(2)}, u32[]{:S(2)}) collective-permute-start(bf16[2,640,1408]{2,1,0:T(8,128)(2,1)} %broadcast_select_fusion.1), channel_id=1, source_target_pairs={{224,0},{232,8},{240,16},{248,24},{0,32},{8,40},{16,48},{24,56},{3... | collective-permute-start | bytes 10813448 | tf_op jit(solution)/shard_map/ppermute | solution.py:11
  406.9 1.8 copy-start.5
  418.5 303.4 %collective-permute-start = (bf16[2,640,1408]{2,1,0:T(8,128)(2,1)}, bf16[2,640,1408]{2,1,0:T(8,128)(2,1)}, u32[]{:S(2)}, u32[]{:S(2)}) collective-permute-start(bf16[2,640,1408]{2,1,0:T(8,128)(2,1)} %get-tuple-element.121), channel_id=1, source_target_pairs={{192,0},{200,8},{208,16},{216,24},{224,32},{232,40},{240,48},{248,... | collective-permute-start | bytes 10813448 | tf_op jit(solution)/shard_map/while/body/eval_jaxpr/ppermute | solution.py:11
  738.3 81.4 %collective-permute-start = (bf16[2,640,1408]{2,1,0:T(8,128)(2,1)}, bf16[2,640,1408]{2,1,0:T(8,128)(2,1)}, u32[]{:S(2)}, u32[]{:S(2)}) collective-permute-start(bf16[2,640,1408]{2,1,0:T(8,128)(2,1)} %get-tuple-element.121), channel_id=1, source_target_pairs={{192,0},{200,8},{208,16},{216,24},{224,32},{232,40},{240,48},{248,... | collective-permute-start | bytes 10813448 | tf_op jit(solution)/shard_map/while/body/eval_jaxpr/ppermute | solution.py:11
  836.1 80.4 %collective-permute-start = (bf16[2,640,1408]{2,1,0:T(8,128)(2,1)}, bf16[2,640,1408]{2,1,0:T(8,128)(2,1)}, u32[]{:S(2)}, u32[]{:S(2)}) collective-permute-start(bf16[2,640,1408]{2,1,0:T(8,128)(2,1)} %get-tuple-element.121), channel_id=1, source_target_pairs={{192,0},{200,8},{208,16},{216,24},{224,32},{232,40},{240,48},{248,... | collective-permute-start | bytes 10813448 | tf_op jit(solution)/shard_map/while/body/eval_jaxpr/ppermute | solution.py:11
  1064.2 4.1 copy-start.1
  1064.2 5.2 copy-start.4
Sparse Core Ops, SparseCore 0:
  933.1 131.0 all-reduce.1
where the time goes:
time: 1080 us
  waiting for transfers between devices  973 us (90%)
  matrix products  46.7 us (4%)
  other arithmetic  21.3 us (2%)
  local copies, waits for them, and re-layouts  17 us (2%)
  between operations  13.4 us (1%)
    ppermute x6, waiting for transfers between devices, from_behind(): return lax.ppermute(block, axis, route)  842 us
    psum x1, waiting for transfers between devices, local(): unit_grad = lax.psum(partial_value, 'pair')  131 us
    dot_general x4, matrix products, relation_tile(): return jnp.dot(relation, partner[0], preferred_element_type=jnp.float32)  35.5 us
  transfers between devices with their start and end apart: 7, of which 7 were waited for; matrix products, arithmetic and copies ran while one was open for 0% of the time, Pallas kernels for 0%

commit v1 on v0

--- a/solution.py
+++ b/solution.py
@@ -60,7 +60,7 @@
 
     partial_value = tile(partner)
     partner, partial_value = lax.fori_loop(0, block_count - 1, advance, (partner, partial_value))
-    unit_grad = lax.psum(partial_value, "pair")
+    unit_grad = jnp.sum(lax.all_gather(partial_value, "pair"), axis=0)
     return finish_rows(s_scale, s_unit, unit_grad)
 
 

time: 1080 us -> 1280 us (1.19)
  waiting for transfers between devices: 973 us -> 1160 us
    all_gather x0 -> x1, waiting for transfers between devices: none -> 316 us  [local(): unit_grad = jnp.sum(lax.all_gather(partial_value, 'pair'), axis=0)]
    psum x1 -> x0, waiting for transfers between devices: 131 us -> none  [local(): unit_grad = lax.psum(partial_value, 'pair')]
where the time goes in v1:
time: 1280 us
  waiting for transfers between devices  1160 us (91%)
  matrix products  46.9 us (4%)
  other arithmetic  34 us (3%)
  local copies, waits for them, and re-layouts  17 us (1%)
  between operations  13.4 us (1%)
    ppermute x6, waiting for transfers between devices, from_behind(): return lax.ppermute(block, axis, route)  842 us
    all_gather x1, waiting for transfers between devices, local(): unit_grad = jnp.sum(lax.all_gather(partial_value, 'pair'), axis=0)  316 us
    dot_general x4, matrix products, relation_tile(): return jnp.dot(relation, partner[0], preferred_element_type=jnp.float32)  35.7 us
  transfers between devices with their start and end apart: 7, of which 7 were waited for; matrix products, arithmetic and copies ran while one was open for 0% of the time, Pallas kernels for 0%

profile of v1, /device:TPU:1, one launch (start us, length us, event | category | flops | bytes accessed | tf_op | source)
XLA Modules:
  0.0 1276.3 jit_solution(17510464556540170291)
XLA Ops:
  6.5 2.5 multiply_reduce_fusion.1
  13.6 2.7 collective-permute-start.1
  16.3 39.4 %collective-permute-done.1 = bf16[2,640,1408]{2,1,0:T(8,128)(2,1)} collective-permute-done((bf16[2,640,1408]{2,1,0:T(8,128)(2,1)}, bf16[2,640,1408]{2,1,0:T(8,128)(2,1)}, u32[]{:S(2)}, u32[]{:S(2)}) %collective-permute-start.1) | collective-permute-done | bytes 3604512 | tf_op jit(solution)/shard_map/ppermute | solution.py:11
  55.8 3.8 broadcast_select_fusion
  60.8 179.3 %collective-permute-done.2 = bf16[2,640,1408]{2,1,0:T(8,128)(2,1)} collective-permute-done((bf16[2,640,1408]{2,1,0:T(8,128)(2,1)}, bf16[2,640,1408]{2,1,0:T(8,128)(2,1)}, u32[]{:S(2)}, u32[]{:S(2)}) %collective-permute-start.2) | collective-permute-done | bytes 3604512 | tf_op jit(solution)/shard_map/ppermute | solution.py:11
  240.2 3.3 broadcast_select_fusion.1
  243.4 161.1 %collective-permute-done.3 = bf16[2,640,1408]{2,1,0:T(8,128)(2,1)} collective-permute-done((bf16[2,640,1408]{2,1,0:T(8,128)(2,1)}, bf16[2,640,1408]{2,1,0:T(8,128)(2,1)}, u32[]{:S(2)}, u32[]{:S(2)}) %collective-permute-start.3) | collective-permute-done | bytes 3604512 | tf_op jit(solution)/shard_map/ppermute | solution.py:11
  410.4 8.1 fusion.11
  418.5 514.6 %while.14 = (s32[]{:T(128)}, bf16[2,640,1408]{2,1,0:T(8,128)(2,1)}, f32[640,1408]{1,0:T(8,128)}, bf16[640,1408]{1,0:T(8,128)(2,1)}, bf16[640,1408]{1,0:T(8,128)(2,1)S(1)}, /*index=5*/s32[]{:T(128)}) while((s32[]{:T(128)}, bf16[2,640,1408]{2,1,0:T(8,128)(2,1)}, f32[640,1408]{1,0:T(8,128)}, bf16[640,1408]{1,0:T(8,128)(2,1)}, ...), condition=%wide.region_3.4_spmd, body=%wide.region_2.3_spmd.sunk | while | flops 3464478720 | bytes 41123948 | solution.py:62
  418.5 303.4 %collective-permute-done = bf16[2,640,1408]{2,1,0:T(8,128)(2,1)} collective-permute-done((bf16[2,640,1408]{2,1,0:T(8,128)(2,1)}, bf16[2,640,1408]{2,1,0:T(8,128)(2,1)}, u32[]{:S(2)}, u32[]{:S(2)}) %collective-permute-start) | collective-permute-done | bytes 3604512 | tf_op jit(solution)/shard_map/while/body/eval_jaxpr/ppermute | solution.py:11
  721.9 4.1 copy.10
  726.0 3.2 fusion.30
  729.2 9.2 convolution_add_fusion.2
  740.6 79.2 %collective-permute-done = bf16[2,640,1408]{2,1,0:T(8,128)(2,1)} collective-permute-done((bf16[2,640,1408]{2,1,0:T(8,128)(2,1)}, bf16[2,640,1408]{2,1,0:T(8,128)(2,1)}, u32[]{:S(2)}, u32[]{:S(2)}) %collective-permute-start) | collective-permute-done | bytes 3604512 | tf_op jit(solution)/shard_map/while/body/eval_jaxpr/ppermute | solution.py:11
  819.7 4.1 copy.10
  823.8 3.2 fusion.30
  827.0 9.2 convolution_add_fusion.2
  837.2 79.5 %collective-permute-done = bf16[2,640,1408]{2,1,0:T(8,128)(2,1)} collective-permute-done((bf16[2,640,1408]{2,1,0:T(8,128)(2,1)}, bf16[2,640,1408]{2,1,0:T(8,128)(2,1)}, u32[]{:S(2)}, u32[]{:S(2)}) %collective-permute-start) | collective-permute-done | bytes 3604512 | tf_op jit(solution)/shard_map/while/body/eval_jaxpr/ppermute | solution.py:11
  916.7 4.1 copy.10
  920.8 3.2 fusion.30
  924.0 9.2 convolution_add_fusion.2
  933.2 315.9 %all-gather.3.cloned.1.call-done = f32[5120,1408]{1,0:T(8,128)} async-done(((f32[640,1408]{1,0:T(8,128)}), f32[5120,1408]{1,0:T(8,128)}) %all-gather.3.cloned.1.call-update) | async-done | bytes 28835856 | tf_op jit(solution)/shard_map/all_gather | solution.py:63
  1249.1 12.7 reduce_sum.38
  1261.8 3.7 multiply_reduce_fusion
  (27 shorter events, 18.9 us)
Async XLA Ops:
  6.5 1242.6 %all-gather.3.cloned.1.call-start = ((), (), s32[]{:S(2)}) async-start(), calls=%async_computation | async-start | bytes 32440320 | tf_op jit(solution)/shard_map/all_gather | solution.py:63
  6.5 3.1 copy-start
  6.5 4.2 copy-start.4
  11.2 2.4 copy-start.3
  13.6 42.1 %collective-permute-start.1 = (bf16[2,640,1408]{2,1,0:T(8,128)(2,1)}, bf16[2,640,1408]{2,1,0:T(8,128)(2,1)}, u32[]{:S(2)}, u32[]{:S(2)}) collective-permute-start(bf16[2,640,1408]{2,1,0:T(8,128)(2,1)} %pad_maximum_fusion), channel_id=1, source_target_pairs={{248,0},{0,8},{8,16},{16,24},{24,32},{32,40},{40,48},{48,56},{56,6... | collective-permute-start | bytes 10813448 | tf_op jit(solution)/shard_map/ppermute | solution.py:11
  59.5 180.6 %collective-permute-start.2 = (bf16[2,640,1408]{2,1,0:T(8,128)(2,1)}, bf16[2,640,1408]{2,1,0:T(8,128)(2,1)}, u32[]{:S(2)}, u32[]{:S(2)}) collective-permute-start(bf16[2,640,1408]{2,1,0:T(8,128)(2,1)} %broadcast_select_fusion), channel_id=1, source_target_pairs={{240,0},{248,8},{0,16},{8,24},{16,32},{24,40},{32,48},{40,56},{48,... | collective-permute-start | bytes 10813448 | tf_op jit(solution)/shard_map/ppermute | solution.py:11
  243.4 161.1 %collective-permute-start.3 = (bf16[2,640,1408]{2,1,0:T(8,128)(2,1)}, bf16[2,640,1408]{2,1,0:T(8,128)(2,1)}, u32[]{:S(2)}, u32[]{:S(2)}) collective-permute-start(bf16[2,640,1408]{2,1,0:T(8,128)(2,1)} %broadcast_select_fusion.1), channel_id=1, source_target_pairs={{224,0},{232,8},{240,16},{248,24},{0,32},{8,40},{16,48},{24,56},{3... | collective-permute-start | bytes 10813448 | tf_op jit(solution)/shard_map/ppermute | solution.py:11
  406.9 1.8 copy-start.5
  418.5 303.4 %collective-permute-start = (bf16[2,640,1408]{2,1,0:T(8,128)(2,1)}, bf16[2,640,1408]{2,1,0:T(8,128)(2,1)}, u32[]{:S(2)}, u32[]{:S(2)}) collective-permute-start(bf16[2,640,1408]{2,1,0:T(8,128)(2,1)} %get-tuple-element.121), channel_id=1, source_target_pairs={{192,0},{200,8},{208,16},{216,24},{224,32},{232,40},{240,48},{248,... | collective-permute-start | bytes 10813448 | tf_op jit(solution)/shard_map/while/body/eval_jaxpr/ppermute | solution.py:11
  738.4 81.4 %collective-permute-start = (bf16[2,640,1408]{2,1,0:T(8,128)(2,1)}, bf16[2,640,1408]{2,1,0:T(8,128)(2,1)}, u32[]{:S(2)}, u32[]{:S(2)}) collective-permute-start(bf16[2,640,1408]{2,1,0:T(8,128)(2,1)} %get-tuple-element.121), channel_id=1, source_target_pairs={{192,0},{200,8},{208,16},{216,24},{224,32},{232,40},{240,48},{248,... | collective-permute-start | bytes 10813448 | tf_op jit(solution)/shard_map/while/body/eval_jaxpr/ppermute | solution.py:11
  836.2 80.5 %collective-permute-start = (bf16[2,640,1408]{2,1,0:T(8,128)(2,1)}, bf16[2,640,1408]{2,1,0:T(8,128)(2,1)}, u32[]{:S(2)}, u32[]{:S(2)}) collective-permute-start(bf16[2,640,1408]{2,1,0:T(8,128)(2,1)} %get-tuple-element.121), channel_id=1, source_target_pairs={{192,0},{200,8},{208,16},{216,24},{224,32},{232,40},{240,48},{248,... | collective-permute-start | bytes 10813448 | tf_op jit(solution)/shard_map/while/body/eval_jaxpr/ppermute | solution.py:11
  1261.8 4.1 copy-start.1
  1261.8 5.2 copy-start.2
Sparse Core Ops, SparseCore 0:
  933.3 315.7 all-gather.2
